TPU v7x, 32 devices: a whole 2x2x4 slice. The times are simulated.
32 devices in a mesh: dp: 8 (over y, x, core), mp: 4 (over z).
Axes of the slice: x: 2, y: 2, z: 4, core: 2. Of those that a mesh axis runs over, the one named last changes fastest.
Arguments:
- response_query: bfloat16 [384, 8, 6144], P('dp', None, 'mp'), may hold values from -80 to 80, as said below
- response_keys: bfloat16 [2, 384, 8, 768], P(None, 'dp'), may hold values from -8 to 8
- prompt_cache: bfloat16 [2, 8, 1024, 768], P(None, 'dp'), may hold values from -6 to 6
- lengths: int32 [384], P('dp'), may hold values from 1 to 8, as said below
- owners: int32 [384], P('dp'), may hold values from 0 to 7, as said below
- pairing: int32 [384], replicated, may hold values from 0 to 383, each once
- residual: bfloat16 [384, 8192], P(None, 'dp'), may hold values from -90 to 90
- output_weight: bfloat16 [6144, 8192], P('mp', 'dp'), may hold values from -0.3125 to 0.3125
- norm_gain: float32 [8192], P('dp'), may hold values from 0.1 to 1.9
- reward_head: float32 [8192], P('dp'), may hold values from -0.0625 to 0.0625
Outputs:
- attention_rows: bfloat16 [384, 8, 6144], P('dp', None, 'mp')
- rewards: float32 [384], replicated
- pair_loss: float32 [], replicated
- weight_gradient: float32 [6144, 8192], P('mp', 'dp')
- head_gradient: float32 [8192], P('dp')
- pooled_gradient: float32 [384, 6144], P('dp', 'mp')
Inputs may be any that keep to these rules, and one draw needn't show every extreme that they name: `response_query`: drawn jointly with response_keys. `lengths`: every dp index holds a response of length 8. The responses of one dp index spread over owners as evenly as possible: each owner receives at most 6 of them, and some owner receives exactly 6.
All inputs are finite; a program needn't handle non-finite values.
Results may differ from a plain program's by a relative error of at most 0.0056.
Values may be sent and summed in bfloat16 or wider, within the bound.
A program may use at most 64 MiB of HBM per device.

v0:
```python
import math
import jax
import jax.numpy as jnp
from jax import lax
from jax.sharding import PartitionSpec as P

D = 8192
HD = 128
Q_HEADS = 48
KV_HEADS = 6
EPSILON = 1e-05


def bradley_terry(rewards, pairing):
    chosen = pairing[0::2]
    rejected = pairing[1::2]
    margin = rewards[chosen] - rewards[rejected]
    loss_value = jnp.mean(jax.nn.softplus(-margin))
    slope = -jax.nn.sigmoid(-margin) / margin.shape[0]
    reward_slope = jnp.zeros_like(rewards).at[chosen].add(slope).at[rejected].add(-slope)
    return (loss_value, reward_slope)


def shards(
    response_query,
    response_keys,
    prompt_cache,
    lengths,
    owners,
    pairing,
    residual,
    output_weight,
    norm_gain,
    reward_head,
):
    groups = lax.axis_size("dp")
    model_rank = lax.axis_index("mp")
    held_count = response_query.shape[0]
    slot_count = response_query.shape[1]
    head_width = response_query.shape[2]
    local_heads = head_width // HD
    group_size = Q_HEADS // KV_HEADS
    per_owner = (held_count + groups - 1) // groups
    if group_size % local_heads == 0:
        window = 1
    elif local_heads % group_size == 0:
        window = local_heads // group_size
    else:
        window = min(KV_HEADS, (local_heads - 1) // group_size + 2)
    first_head = jnp.minimum(model_rank * local_heads // group_size, KV_HEADS - window)
    head_slot = (model_rank * local_heads + jnp.arange(local_heads)) // group_size - first_head
    score_scale = 1.0 / math.sqrt(HD)
    own_window = lax.dynamic_slice_in_dim(response_keys, first_head * HD, window * HD, 3)
    spread = own_window.reshape(2, held_count, slot_count, window, HD)
    picked = jnp.take(spread, head_slot, axis=3).reshape(
        2, held_count, slot_count, local_heads * HD
    )
    key_pick = jnp.arange(local_heads)
    outgoing_keys = jnp.concatenate([picked[0], picked[1]], axis=-1)
    positions = jnp.arange(held_count)
    earlier = (owners[None, :] == owners[:, None]) & (positions[None, :] < positions[:, None])
    target = owners * per_owner + jnp.sum(earlier, axis=1)
    capacity = groups * per_owner
    query_buffer = (
        jnp.zeros((capacity, slot_count, head_width), jnp.bfloat16).at[target].set(response_query)
    )
    query_buffer = query_buffer.reshape(groups, per_owner, slot_count, head_width)
    key_buffer = (
        jnp.zeros((capacity, slot_count, 2 * local_heads * HD), jnp.bfloat16)
        .at[target]
        .set(outgoing_keys)
    )
    key_buffer = key_buffer.reshape(groups, per_owner, slot_count, 2 * local_heads * HD)
    length_buffer = (
        jnp.zeros((capacity,), jnp.int32).at[target].set(lengths).reshape(groups, per_owner)
    )
    prefix = lax.dynamic_slice_in_dim(prompt_cache[:, 0], first_head * HD, window * HD, 2)
    query_in = lax.all_to_all(query_buffer, "dp", split_axis=0, concat_axis=0, tiled=True)
    keys_in = lax.all_to_all(key_buffer, "dp", split_axis=0, concat_axis=0, tiled=True)
    length_in = lax.all_to_all(length_buffer, "dp", split_axis=0, concat_axis=0, tiled=True)
    sources = query_in.shape[0]
    item_count = query_in.shape[1]
    blocks = sources * item_count
    row_count = blocks * slot_count
    queries = query_in.reshape(blocks, slot_count, local_heads, HD)
    own_keys = keys_in.reshape(blocks, slot_count, 2, local_heads, HD)
    live_length = length_in.reshape(blocks)
    offsets = jnp.arange(slot_count)
    allowed = (offsets[None, None, :] <= offsets[None, :, None]) & (
        offsets[None, None, :] < live_length[:, None, None]
    )
    valid_rows = offsets[None, :] < live_length[:, None]

    def one_head(head_index):
        query_head = lax.dynamic_index_in_dim(queries, head_index, 2, keepdims=False)
        self_pair = lax.dynamic_index_in_dim(own_keys, key_pick[head_index], 3, keepdims=False)
        cache_pair = lax.dynamic_slice_in_dim(prefix, head_slot[head_index] * HD, HD, 2)
        flat_query = query_head.reshape(row_count, HD)
        far_scores = (
            lax.dot_general(
                flat_query,
                cache_pair[0],
                (((1,), (1,)), ((), ())),
                preferred_element_type=jnp.float32,
            )
            * score_scale
        )
        near_scores = (
            jnp.einsum(
                "bth,bsh->bts", query_head, self_pair[:, :, 0], preferred_element_type=jnp.float32
            )
            * score_scale
        )
        near_scores = jnp.where(allowed, near_scores, -jnp.inf)
        row_top = jnp.maximum(
            jnp.max(far_scores, axis=1).reshape(blocks, slot_count), jnp.max(near_scores, axis=2)
        )
        far_weight = jnp.exp(far_scores - row_top.reshape(row_count, 1))
        near_weight = jnp.exp(near_scores - row_top[:, :, None])
        weight_total = jnp.sum(far_weight, axis=1).reshape(blocks, slot_count) + jnp.sum(
            near_weight, axis=2
        )
        output = jnp.dot(
            far_weight.astype(jnp.bfloat16), cache_pair[1], preferred_element_type=jnp.float32
        ).reshape(blocks, slot_count, HD)
        output = output + jnp.einsum(
            "bts,bsh->bth",
            near_weight.astype(jnp.bfloat16),
            self_pair[:, :, 1],
            preferred_element_type=jnp.float32,
        )
        output = output / weight_total[:, :, None]
        return jnp.where(valid_rows[:, :, None], output, 0.0).astype(jnp.bfloat16)

    heads_out = lax.map(one_head, jnp.arange(local_heads))
    result = jnp.transpose(heads_out, (1, 2, 0, 3)).reshape(
        sources, item_count, slot_count, head_width
    )
    returned = lax.all_to_all(result, "dp", split_axis=0, concat_axis=0, tiled=True)
    attention_rows = returned.reshape(capacity, slot_count, head_width)[target]
    pooled_local = attention_rows[positions, lengths - 1]
    pooled_all = lax.all_gather(pooled_local, "dp", axis=0, tiled=True)
    partial_mix = jnp.dot(pooled_all, output_weight, preferred_element_type=jnp.float32)
    scaled_head = norm_gain * reward_head
    combined = lax.psum(partial_mix, "mp") + residual.astype(jnp.float32)
    square_sum = jnp.sum(combined * combined, axis=1)
    signal = jnp.sum(combined * scaled_head[None, :], axis=1)
    square_sum, signal = lax.psum((square_sum, signal), "dp")
    inverse = lax.rsqrt(square_sum / D + EPSILON)
    rewards = inverse * signal
    pair_loss, reward_slope = bradley_terry(rewards, pairing)
    direct_term = reward_slope * inverse
    norm_term = reward_slope * inverse * inverse * inverse * signal / D
    upstream = direct_term[:, None] * scaled_head[None, :] - norm_term[:, None] * combined
    head_gradient = jnp.sum(direct_term[:, None] * combined * norm_gain[None, :], axis=0)
    upstream_half = upstream.astype(jnp.bfloat16)
    weight_gradient = lax.dot_general(
        pooled_all, upstream_half, (((0,), (0,)), ((), ())), preferred_element_type=jnp.float32
    )
    pooled_gradient = lax.psum_scatter(
        lax.dot_general(
            upstream_half,
            output_weight,
            (((1,), (1,)), ((), ())),
            preferred_element_type=jnp.float32,
        ),
        "dp",
        scatter_dimension=0,
        tiled=True,
    )
    return (attention_rows, rewards, pair_loss, weight_gradient, head_gradient, pooled_gradient)


def solution(mesh):
    placed = (
        P("dp", None, "mp"),
        P(None, "dp", None, None),
        P(None, "dp", None, None),
        P("dp"),
        P("dp"),
        P(),
        P(None, "dp"),
        P("mp", "dp"),
        P("dp"),
        P("dp"),
    )
    return jax.shard_map(
        shards,
        mesh=mesh,
        in_specs=placed,
        out_specs=(P("dp", None, "mp"), P(), P(), P("mp", "dp"), P("dp"), P("dp", "mp")),
        check_vma=False,
    )
```

profile of v0, /device:TPU:0, one launch (start us, length us, event | category | flops | bytes accessed | tf_op | source)
XLA Modules:
  0.0 529.6 jit_solution(9194661605754231046)
XLA Ops:
  10.4 5.2 all-to-all-start
  16.2 1.9 dynamic-slice_bitcast_fusion.5
  18.1 3.6 gather_fusion
  21.8 3.4 select_bitcast_fusion
  26.2 7.2 %scatter_fusion = bf16[48,8,1536]{2,1,0:T(8,128)(2,1)} fusion(bf16[48,8,1536]{2,1,0:T(8,128)(2,1)} %broadcast_in_dim.88, s32[48]{0:T(128)S(1)} %compare_select_fusion.6, bf16[48,8,1536]{2,1,0:T(8,128)(2,1)} %param.12), kind=kCustom, calls=%fused_computation.6 | custom fusion | bytes 3539136 | tf_op jit(solution)/shard_map/scatter | solution.py:65
  33.4 4.2 all-to-all-start.1
  37.7 1.8 fusion.43
  43.2 8.2 %scatter_fusion.1 = bf16[48,8,3072]{2,1,0:T(8,128)(2,1)} fusion(bf16[48,8,3072]{2,1,0:T(8,128)(2,1)} %broadcast_in_dim.89, s32[48]{0:T(128)S(1)} %compare_select_fusion.6, bf16[48,8,3072]{2,1,0:T(8,128)(2,1)} %pad_maximum_fusion), kind=kCustom, calls=%fused_computation.7 | custom fusion | bytes 7078080 | tf_op jit(solution)/shard_map/scatter | solution.py:71
  51.4 3.1 all-to-all-done.1
  54.5 4.4 all-to-all-start.2
  58.9 2.7 dynamic-slice_bitcast_fusion.4
  62.9 25.4 %all-to-all-done.2 = bf16[8,6,8,3072]{3,2,1,0:T(8,128)(2,1)} async-done(((bf16[8,6,8,3072]{3,2,1,0:T(8,128)(2,1)}), bf16[8,6,8,3072]{3,2,1,0:T(8,128)(2,1)}, u32[]{:S(2)}, u32[]{:S(2)}) %all-to-all-start.2) | async-done | bytes 2359328 | tf_op jit(solution)/shard_map/all_to_all | solution.py:79
  88.9 239.0 %while.13 = (s32[]{:T(128)}, bf16[12,48,8,128]{3,2,0,1:T(8,128)(2,1)}, s32[12]{0:T(128)}, bf16[48,8,12,128]{3,1,2,0:T(8,128)(2,1)}, s32[12]{0:T(128)}, /*index=5...) while((s32[]{:T(128)}, ...), condition=%wide.region_9.10_spmd.clone.clone, body=%wide.region_4.9_spmd.clone.clone.sunk | while | flops 205486080 | bytes 6827307 | solution.py:135
  94.0 2.5 fusion.67
  103.6 1.8 fusion.72
  106.0 1.9 fusion.70
  113.9 2.5 fusion.67
  123.5 1.8 fusion.72
  126.0 1.9 fusion.70
  133.8 2.5 fusion.67
  143.4 1.8 fusion.72
  145.9 1.9 fusion.70
  153.7 2.5 fusion.67
  163.3 1.8 fusion.72
  165.8 1.9 fusion.70
  173.7 2.5 fusion.67
  183.3 1.8 fusion.72
  185.7 1.9 fusion.70
  193.6 2.5 fusion.67
  203.2 1.8 fusion.72
  205.6 1.9 fusion.70
  213.5 2.5 fusion.67
  223.1 1.8 fusion.72
  225.6 1.9 fusion.70
  233.4 2.5 fusion.67
  243.0 1.8 fusion.72
  245.5 1.9 fusion.70
  253.3 2.5 fusion.67
  263.0 1.8 fusion.72
  265.4 1.9 fusion.70
  273.3 2.5 fusion.67
  282.9 1.8 fusion.72
  285.3 1.9 fusion.70
  293.2 2.5 fusion.67
  302.8 1.8 fusion.72
  305.2 1.9 fusion.70
  313.1 2.5 fusion.67
  322.7 1.8 fusion.72
  325.2 1.9 fusion.70
  327.9 4.4 all-to-all-start.3
  332.4 16.7 %all-to-all-done.3 = bf16[8,6,8,1536]{3,2,1,0:T(8,128)(2,1)} async-done(((bf16[8,6,8,1536]{3,2,1,0:T(8,128)(2,1)}), bf16[8,6,8,1536]{3,2,1,0:T(8,128)(2,1)}, u32[]{:S(2)}, u32[]{:S(2)}) %all-to-all-start.3) | async-done | bytes 1179680 | tf_op jit(solution)/shard_map/all_to_all | solution.py:139
  349.2 3.0 gather_fusion.1
  352.1 3.2 gather_fusion.2
  355.4 23.6 %all-gather.2.cloned.1.call-done = bf16[384,1536]{1,0:T(8,128)(2,1)} async-done(((bf16[48,1536]{1,0:T(8,128)(2,1)}), bf16[384,1536]{1,0:T(8,128)(2,1)}) %all-gather.2.cloned.1.call-update) | async-done | bytes 1179664 | tf_op jit(solution)/shard_map/all_gather | solution.py:142
  378.9 3.8 fusion.44
  383.9 68.1 %all-reduce.3.cloned.1.call-done = f32[384,1024]{1,0:T(8,128)} async-done(((f32[384,1024]{1,0:T(8,128)}), f32[384,1024]{1,0:T(8,128)}) %all-reduce.3.cloned.1.call-update) | async-done | bytes 1572880 | tf_op jit(solution)/shard_map/psum | solution.py:145
  452.0 2.0 multiply_reduce_fusion.2
  454.0 12.5 %all-reduce = (f32[384]{0:T(512)S(1)}, f32[384]{0:T(512)S(1)}) all-reduce(f32[384]{0:T(512)S(1)} %get-tuple-element.190, f32[384]{0:T(512)S(1)} %get-tuple-element.189), channel_id=1, replica_groups=mesh['dp'=8,'mp'=4] {'dp'}, use_global_device_ids=true, to_apply=%region_14.15 | all-reduce | flops 768 | bytes 6144 | tf_op jit(solution)/shard_map/psum | solution.py:148
  470.4 1.9 scatter_custom_fusion.3
  472.3 2.0 scatter_fusion.2
  474.4 2.7 multiply_reduce_fusion
  477.9 2.9 fusion.46
  481.5 6.0 %fusion.45 = f32[1536,1024]{1,0:T(8,128)} fusion(bf16[384,1536]{1,0:T(8,128)(2,1)} %all-gather.2.cloned.1.call-done, bf16[384,1024]{1,0:T(8,128)(2,1)} %copy-done.3), kind=kOutput, calls=%fused_computation.102 | convolution fusion | flops 1207959552 | bytes 8257536 | tf_op jit(solution)/shard_map/dot_general | solution.py:157
  487.5 34.5 %reduce-scatter.2.cloned.1.call-done = f32[48,1536]{1,0:T(8,128)} async-done(((f32[384,1536]{1,0:T(8,128)}), f32[48,1536]{1,0:T(8,128)}) %reduce-scatter.2.cloned.1.call-update) | async-done | bytes 294928 | tf_op jit(solution)/shard_map/reduce_scatter | solution.py:160
  (333 shorter events, 126.2 us)
Async XLA Ops:
  7.2 371.8 %copy-start = (bf16[1536,1024]{1,0:T(8,128)(2,1)S(1)}, bf16[1536,1024]{1,0:T(8,128)(2,1)}, u32[]{:S(2)}) copy-start(bf16[1536,1024]{1,0:T(8,128)(2,1)} %param.19) | copy-start | bytes 9437188
  8.9 34.3 %copy-start.5 = (s32[48]{0:T(128)}, s32[48]{0:T(128)S(1)}, u32[]{:S(2)}) copy-start(s32[48]{0:T(128)S(1)} %compare_select_fusion.6) | copy-start | bytes 580
  10.4 23.0 %all-to-all-start = ((s32[8,1,6]{2,1,0:T(1,128)}), s32[8,1,6]{2,1,0:T(1,128)S(1)}, u32[]{:S(2)}, u32[]{:S(2)}) async-start(s32[8,1,6]{2,1,0:T(1,128)} %bitcast.10), calls=%async_computation | async-start | bytes 8192 | tf_op jit(solution)/shard_map/all_to_all | solution.py:80
  33.4 21.1 %all-to-all-start.1 = ((bf16[8,6,8,1536]{3,2,1,0:T(8,128)(2,1)}), bf16[8,6,8,1536]{3,2,1,0:T(8,128)(2,1)}, u32[]{:S(2)}, u32[]{:S(2)}) async-start(bf16[8,6,8,1536]{3,2,1,0:T(8,128)(2,1)} %bitcast.101), calls=%async_computation.1 | async-start | bytes 2359296 | tf_op jit(solution)/shard_map/all_to_all | solution.py:78
  54.5 33.8 %all-to-all-start.2 = ((bf16[8,6,8,3072]{3,2,1,0:T(8,128)(2,1)}), bf16[8,6,8,3072]{3,2,1,0:T(8,128)(2,1)}, u32[]{:S(2)}, u32[]{:S(2)}) async-start(bf16[8,6,8,3072]{3,2,1,0:T(8,128)(2,1)} %bitcast.100), calls=%async_computation.2 | async-start | bytes 4718592 | tf_op jit(solution)/shard_map/all_to_all | solution.py:79
  102.5 3.2 copy-start.2
  122.4 3.2 copy-start.2
  142.3 3.2 copy-start.2
  162.2 3.2 copy-start.2
  182.2 3.2 copy-start.2
  202.1 3.2 copy-start.2
  222.0 3.2 copy-start.2
  241.9 3.2 copy-start.2
  261.8 3.2 copy-start.2
  281.8 3.2 copy-start.2
  301.7 3.2 copy-start.2
  321.6 3.2 copy-start.2
  327.9 4.4 copy-start.6
  327.9 4.5 copy-start.9
  327.9 21.2 %all-to-all-start.3 = ((bf16[8,6,8,1536]{3,2,1,0:T(8,128)(2,1)}), bf16[8,6,8,1536]{3,2,1,0:T(8,128)(2,1)}, u32[]{:S(2)}, u32[]{:S(2)}) async-start(bf16[8,6,8,1536]{3,2,1,0:T(8,128)(2,1)} %bitcast.12), calls=%async_computation.3 | async-start | bytes 2359296 | tf_op jit(solution)/shard_map/all_to_all | solution.py:139
  332.3 46.6 %all-gather.2.cloned.1.call-start = ((), (), s32[]{:S(2)}) async-start(), calls=%async_computation.5 | async-start | bytes 1327104 | tf_op jit(solution)/shard_map/all_gather | solution.py:142
  355.3 96.7 %all-reduce.3.cloned.1.call-start = ((), (), s32[]{:S(2)}) async-start(), calls=%async_computation.6 | async-start | bytes 3145728 | tf_op jit(solution)/shard_map/psum | solution.py:145
  382.7 0.7 copy-start.8
  382.7 1.1 copy-start.4
  382.7 1.1 copy-start.7
  382.8 139.2 %reduce-scatter.2.cloned.1.call-start = ((), (), s32[]{:S(2)}) async-start(), calls=%async_computation.7 | async-start | bytes 2654208 | tf_op jit(solution)/shard_map/reduce_scatter | solution.py:160
  466.5 7.8 %copy-start.1 = (f32[384]{0:T(512)}, f32[384]{0:T(512)S(1)}, u32[]{:S(2)}) copy-start(f32[384]{0:T(512)S(1)} %fusion.33) | copy-start | bytes 4612
  477.0 0.9 copy-start.3
Sparse Core Ops, SparseCore 0:
  355.4 23.4 all-gather.1
  382.9 69.0 all-reduce.2
  480.9 40.9 reduce-scatter.1
where the time goes:
time: 534 us; the launch traced here: 530 us
  waiting for transfers between devices  171 us (32%)
  local copies, waits for them, and re-layouts  116 us (22%)
  matrix products  88.1 us (16%)
  loops' own time  55.3 us (10%)
  other arithmetic  52 us (10%)
  starting transfers between devices  18.3 us (3%)
  between operations  15.7 us (3%)
  blocking collectives  12.5 us (2%)
    psum x1, waiting for transfers between devices, shards(): combined = lax.psum(partial_mix, 'mp') + residual.astype(jnp.float32)  68.1 us
    another operation x1, loops' own time, shards(): heads_out = lax.map(one_head, jnp.arange(local_heads))  55.3 us
    reduce_scatter x1, waiting for transfers between devices, shards(): lax.psum_scatter(lax.dot_general(upstream_half, output_weight, (((1,), (1...  34.5 us
    dot_general x12, matrix products, one_head(): lax.dot_general(flat_query, cache_pair[0], (((1,), (1,)), ((), ())), pref...  30.3 us
    all_to_all x1, waiting for transfers between devices, shards(): lax.all_to_all(key_buffer, 'dp', split_axis=0, concat_axis=0, tiled=True)  25.4 us
    all_gather x1, waiting for transfers between devices, shards(): pooled_all = lax.all_gather(pooled_local, 'dp', axis=0, tiled=True)  23.6 us
    dot_general x12, matrix products, one_head(): jnp.dot(far_weight.astype(jnp.bfloat16), cache_pair[1], preferred_element...  22.2 us
    reduce_sum x12, other arithmetic, one_head(): jnp.sum(far_weight, axis=1).reshape(blocks, slot_count)  21.4 us
  transfers between devices with their start and end apart: 7, of which 6 were waited for; matrix products, arithmetic and copies ran while one was open for 8% of the time, Pallas kernels for 0%

commit v1 on v0

--- a/solution.py
+++ b/solution.py
@@ -139,7 +139,12 @@
     returned = lax.all_to_all(result, "dp", split_axis=0, concat_axis=0, tiled=True)
     attention_rows = returned.reshape(capacity, slot_count, head_width)[target]
     pooled_local = attention_rows[positions, lengths - 1]
-    pooled_all = lax.all_gather(pooled_local, "dp", axis=0, tiled=True)
+    ring = [pooled_local]
+    for hop in range(7):
+        ring.append(lax.ppermute(ring[-1], "dp", [(dev, (dev + 1) % 8) for dev in range(8)]))
+    pooled_all = jnp.roll(
+        jnp.concatenate(ring[::-1], axis=0), (lax.axis_index("dp") + 1) * ring[0].shape[0], axis=0
+    )
     partial_mix = jnp.dot(pooled_all, output_weight, preferred_element_type=jnp.float32)
     scaled_head = norm_gain * reward_head
     combined = lax.psum(partial_mix, "mp") + residual.astype(jnp.float32)

time: 534 us -> 568 us (1.064)
  waiting for transfers between devices: 171 us -> 186 us
  local copies, waits for them, and re-layouts: 116 us -> 126 us
  other arithmetic: 52 us -> 60.3 us
    ppermute x0 -> x7, waiting for transfers between devices: none -> 38.6 us  [shards(): lax.ppermute(ring[-1], 'dp', [(dev, (dev + 1) % 8) for dev in range(8)])]
    all_gather x1 -> x0, waiting for transfers between devices: 23.6 us -> none  [shards(): pooled_all = lax.all_gather(pooled_local, 'dp', axis=0, tiled=True)]
    unnamed x18 -> x51, local copies, waits for them, and re-layouts: 1.52 us -> 12.4 us
    reduce_sum x12, other arithmetic: 1.24 us -> 10.4 us  [one_head(): jnp.sum(near_weight, axis=2)]
  transfers between devices with their start and end apart: 7 -> 13, of which waited for: 6 -> 12; matrix products, arithmetic and copies ran while one was open for 8% -> 7% of each run, Pallas kernels for 0% -> 0%
where the time goes in v1:
time: 568 us; the launch traced here: 562 us
  waiting for transfers between devices  186 us (33%)
  local copies, waits for them, and re-layouts  126 us (22%)
  matrix products  86.9 us (15%)
  other arithmetic  60.3 us (11%)
  loops' own time  55.3 us (10%)
  starting transfers between devices  18.3 us (3%)
  between operations  16.2 us (3%)
  blocking collectives  12.5 us (2%)
    psum x1, waiting for transfers between devices, shards(): combined = lax.psum(partial_mix, 'mp') + residual.astype(jnp.float32)  68.1 us
    another operation x1, loops' own time, shards(): heads_out = lax.map(one_head, jnp.arange(local_heads))  55.3 us
    ppermute x7, waiting for transfers between devices, shards(): lax.ppermute(ring[-1], 'dp', [(dev, (dev + 1) % 8) for dev in range(8)])  38.6 us
    reduce_scatter x1, waiting for transfers between devices, shards(): lax.psum_scatter(lax.dot_general(upstream_half, output_weight, (((1,), (1...  34.4 us
    dot_general x12, matrix products, one_head(): lax.dot_general(flat_query, cache_pair[0], (((1,), (1,)), ((), ())), pref...  30.3 us
    all_to_all x1, waiting for transfers between devices, shards(): lax.all_to_all(key_buffer, 'dp', split_axis=0, concat_axis=0, tiled=True)  25.4 us
    dot_general x12, matrix products, one_head(): jnp.dot(far_weight.astype(jnp.bfloat16), cache_pair[1], preferred_element...  22.2 us
    reduce_sum x12, other arithmetic, one_head(): jnp.sum(far_weight, axis=1).reshape(blocks, slot_count)  21.4 us
  transfers between devices with their start and end apart: 13, of which 12 were waited for; matrix products, arithmetic and copies ran while one was open for 7% of the time, Pallas kernels for 0%

profile of v1, /device:TPU:0, one launch (start us, length us, event | category | flops | bytes accessed | tf_op | source)
XLA Modules:
  0.0 562.1 jit_solution(10637267111217814411)
XLA Ops:
  10.4 5.2 all-to-all-start
  16.2 1.9 dynamic-slice_bitcast_fusion.5
  18.1 3.6 gather_fusion
  21.8 3.4 select_bitcast_fusion
  26.2 7.2 %scatter_fusion = bf16[48,8,1536]{2,1,0:T(8,128)(2,1)} fusion(bf16[48,8,1536]{2,1,0:T(8,128)(2,1)} %broadcast_in_dim.88, s32[48]{0:T(128)S(1)} %compare_select_fusion.6, bf16[48,8,1536]{2,1,0:T(8,128)(2,1)} %param.12), kind=kCustom, calls=%fused_computation.6 | custom fusion | bytes 3539136 | tf_op jit(solution)/shard_map/scatter | solution.py:65
  33.4 4.2 all-to-all-start.1
  37.7 1.8 fusion.49
  43.2 8.2 %scatter_fusion.1 = bf16[48,8,3072]{2,1,0:T(8,128)(2,1)} fusion(bf16[48,8,3072]{2,1,0:T(8,128)(2,1)} %broadcast_in_dim.89, s32[48]{0:T(128)S(1)} %compare_select_fusion.6, bf16[48,8,3072]{2,1,0:T(8,128)(2,1)} %pad_maximum_fusion), kind=kCustom, calls=%fused_computation.7 | custom fusion | bytes 7078080 | tf_op jit(solution)/shard_map/scatter | solution.py:71
  51.4 3.1 all-to-all-done.1
  54.5 4.4 all-to-all-start.2
  58.9 2.7 dynamic-slice_bitcast_fusion.4
  62.9 25.4 %all-to-all-done.2 = bf16[8,6,8,3072]{3,2,1,0:T(8,128)(2,1)} async-done(((bf16[8,6,8,3072]{3,2,1,0:T(8,128)(2,1)}), bf16[8,6,8,3072]{3,2,1,0:T(8,128)(2,1)}, u32[]{:S(2)}, u32[]{:S(2)}) %all-to-all-start.2) | async-done | bytes 2359328 | tf_op jit(solution)/shard_map/all_to_all | solution.py:79
  88.9 247.1 %while.13 = (s32[]{:T(128)}, bf16[12,48,8,128]{3,2,0,1:T(8,128)(2,1)}, s32[12]{0:T(128)}, bf16[48,8,12,128]{3,1,2,0:T(8,128)(2,1)}, s32[12]{0:T(128)}, /*index=5...) while((s32[]{:T(128)}, ...), condition=%wide.region_9.10_spmd.clone.clone, body=%wide.region_4.9_spmd.clone.clone.sunk | while | flops 205486080 | bytes 6778127 | solution.py:135
  94.0 2.5 fusion.69
  103.5 1.8 fusion.74
  106.7 1.9 fusion.72
  114.6 2.5 fusion.69
  124.1 1.8 fusion.74
  127.3 1.9 fusion.72
  135.2 2.5 fusion.69
  144.7 1.8 fusion.74
  147.9 1.9 fusion.72
  155.8 2.5 fusion.69
  165.3 1.8 fusion.74
  168.5 1.9 fusion.72
  176.3 2.5 fusion.69
  185.9 1.8 fusion.74
  189.1 1.9 fusion.72
  196.9 2.5 fusion.69
  206.5 1.8 fusion.74
  209.7 1.9 fusion.72
  217.5 2.5 fusion.69
  230.3 1.9 fusion.72
  238.1 2.5 fusion.69
  250.9 1.9 fusion.72
  258.7 2.5 fusion.69
  271.5 1.9 fusion.72
  279.3 2.5 fusion.69
  292.0 1.9 fusion.72
  299.9 2.5 fusion.69
  312.6 1.9 fusion.72
  320.5 2.5 fusion.69
  333.2 1.9 fusion.72
  336.0 4.4 all-to-all-start.3
  340.5 16.7 %all-to-all-done.3 = bf16[8,6,8,1536]{3,2,1,0:T(8,128)(2,1)} async-done(((bf16[8,6,8,1536]{3,2,1,0:T(8,128)(2,1)}), bf16[8,6,8,1536]{3,2,1,0:T(8,128)(2,1)}, u32[]{:S(2)}, u32[]{:S(2)}) %all-to-all-start.3) | async-done | bytes 1179680 | tf_op jit(solution)/shard_map/all_to_all | solution.py:139
  357.2 3.0 gather_fusion.1
  360.2 2.4 gather_fusion.2
  362.7 5.5 collective-permute-done
  368.1 5.5 collective-permute-done.1
  374.3 5.5 collective-permute-done.2
  380.4 5.5 collective-permute-done.3
  386.5 5.5 collective-permute-done.4
  392.6 5.6 collective-permute-done.5
  398.2 5.8 %collective-permute-done.6 = bf16[48,1536]{1,0:T(8,128)(2,1)} collective-permute-done((bf16[48,1536]{1,0:T(8,128)(2,1)}, bf16[48,1536]{1,0:T(8,128)(2,1)}, u32[]{:S(2)}, u32[]{:S(2)}) %collective-permute-start.6) | collective-permute-done | bytes 147488 | tf_op jit(solution)/shard_map/ppermute | solution.py:144
  413.0 2.5 fusion.28
  416.1 68.1 %all-reduce.3.cloned.1.call-done = f32[384,1024]{1,0:T(8,128)} async-done(((f32[384,1024]{1,0:T(8,128)}), f32[384,1024]{1,0:T(8,128)}) %all-reduce.3.cloned.1.call-update) | async-done | bytes 1572880 | tf_op jit(solution)/shard_map/psum | solution.py:150
  484.2 2.0 multiply_reduce_fusion.2
  486.2 12.5 %all-reduce = (f32[384]{0:T(512)S(1)}, f32[384]{0:T(512)S(1)}) all-reduce(f32[384]{0:T(512)S(1)} %get-tuple-element.190, f32[384]{0:T(512)S(1)} %get-tuple-element.189), channel_id=1, replica_groups=mesh['dp'=8,'mp'=4] {'dp'}, use_global_device_ids=true, to_apply=%region_14.15 | all-reduce | flops 768 | bytes 6144 | tf_op jit(solution)/shard_map/psum | solution.py:153
  502.6 2.0 scatter_custom_fusion.3
  504.6 1.9 scatter_fusion.2
  506.5 2.7 multiply_reduce_fusion
  510.1 2.9 fusion.50
  513.7 6.0 %fusion.26 = f32[1536,1024]{1,0:T(8,128)} fusion(bf16[384,1024]{1,0:T(8,128)(2,1)} %copy-done.2, bf16[768,1536]{1,0:T(8,128)(2,1)} %copy-done.3, s32[]{:T(128)S(6)} %select_n.114), kind=kOutput, calls=%fused_computation.55 | convolution fusion | flops 1207959552 | bytes 8257540 | tf_op jit(solution)/shard_map/dot_general | solution.py:162
  519.7 34.4 %reduce-scatter.2.cloned.1.call-done = f32[48,1536]{1,0:T(8,128)} async-done(((f32[384,1536]{1,0:T(8,128)}), f32[48,1536]{1,0:T(8,128)}) %reduce-scatter.2.cloned.1.call-update) | async-done | bytes 294928 | tf_op jit(solution)/shard_map/reduce_scatter | solution.py:165
  (353 shorter events, 155.9 us)
Async XLA Ops:
  7.2 405.8 %copy-start = (bf16[1536,1024]{1,0:T(8,128)(2,1)S(1)}, bf16[1536,1024]{1,0:T(8,128)(2,1)}, u32[]{:S(2)}) copy-start(bf16[1536,1024]{1,0:T(8,128)(2,1)} %param.19) | copy-start | bytes 9437188
  8.9 34.3 %copy-start.13 = (s32[48]{0:T(128)}, s32[48]{0:T(128)S(1)}, u32[]{:S(2)}) copy-start(s32[48]{0:T(128)S(1)} %compare_select_fusion.6) | copy-start | bytes 580
  10.4 23.0 %all-to-all-start = ((s32[8,1,6]{2,1,0:T(1,128)}), s32[8,1,6]{2,1,0:T(1,128)S(1)}, u32[]{:S(2)}, u32[]{:S(2)}) async-start(s32[8,1,6]{2,1,0:T(1,128)} %bitcast.10), calls=%async_computation | async-start | bytes 8192 | tf_op jit(solution)/shard_map/all_to_all | solution.py:80
  33.4 21.1 %all-to-all-start.1 = ((bf16[8,6,8,1536]{3,2,1,0:T(8,128)(2,1)}), bf16[8,6,8,1536]{3,2,1,0:T(8,128)(2,1)}, u32[]{:S(2)}, u32[]{:S(2)}) async-start(bf16[8,6,8,1536]{3,2,1,0:T(8,128)(2,1)} %bitcast.99), calls=%async_computation.1 | async-start | bytes 2359296 | tf_op jit(solution)/shard_map/all_to_all | solution.py:78
  54.5 33.8 %all-to-all-start.2 = ((bf16[8,6,8,3072]{3,2,1,0:T(8,128)(2,1)}), bf16[8,6,8,3072]{3,2,1,0:T(8,128)(2,1)}, u32[]{:S(2)}, u32[]{:S(2)}) async-start(bf16[8,6,8,3072]{3,2,1,0:T(8,128)(2,1)} %bitcast.98), calls=%async_computation.2 | async-start | bytes 4718592 | tf_op jit(solution)/shard_map/all_to_all | solution.py:79
  336.0 4.4 copy-start.14
  336.0 4.5 copy-start.17
  336.0 21.2 %all-to-all-start.3 = ((bf16[8,6,8,1536]{3,2,1,0:T(8,128)(2,1)}), bf16[8,6,8,1536]{3,2,1,0:T(8,128)(2,1)}, u32[]{:S(2)}, u32[]{:S(2)}) async-start(bf16[8,6,8,1536]{3,2,1,0:T(8,128)(2,1)} %bitcast.100), calls=%async_computation.3 | async-start | bytes 2359296 | tf_op jit(solution)/shard_map/all_to_all | solution.py:139
  340.4 143.8 %all-reduce.3.cloned.1.call-start = ((), (), s32[]{:S(2)}) async-start(), calls=%async_computation.5 | async-start | bytes 3145728 | tf_op jit(solution)/shard_map/psum | solution.py:150
  362.6 5.5 collective-permute-start
  368.1 5.5 collective-permute-start.1
  373.6 0.7 copy-start.4
  374.3 5.5 collective-permute-start.2
  379.7 0.6 copy-start.6
  380.4 5.5 collective-permute-start.3
  385.8 0.7 copy-start.8
  386.5 5.5 collective-permute-start.4
  392.0 0.7 copy-start.10
  392.6 5.6 collective-permute-start.5
  398.2 5.8 %collective-permute-start.6 = (bf16[48,1536]{1,0:T(8,128)(2,1)}, bf16[48,1536]{1,0:T(8,128)(2,1)}, u32[]{:S(2)}, u32[]{:S(2)}) collective-permute-start(bf16[48,1536]{1,0:T(8,128)(2,1)} %collective-permute-done.5), channel_id=1, source_target_pairs={{0,4},{4,8},{8,12},{12,16},{16,20},{20,24},{24,28},{28,0},{1,5},{5... | collective-permute-start | bytes 442376 | tf_op jit(solution)/shard_map/ppermute | solution.py:144
  398.2 13.2 %copy-start.11 = (bf16[48,1536]{1,0:T(8,128)(2,1)S(1)}, bf16[48,1536]{1,0:T(8,128)(2,1)}, u32[]{:S(2)}) copy-start(bf16[48,1536]{1,0:T(8,128)(2,1)} %copy-done.10) | copy-start | bytes 442372
  398.2 13.2 %copy-start.9 = (bf16[48,1536]{1,0:T(8,128)(2,1)S(1)}, bf16[48,1536]{1,0:T(8,128)(2,1)}, u32[]{:S(2)}) copy-start(bf16[48,1536]{1,0:T(8,128)(2,1)} %copy-done.8) | copy-start | bytes 442372
  398.2 13.3 %copy-start.7 = (bf16[48,1536]{1,0:T(8,128)(2,1)S(1)}, bf16[48,1536]{1,0:T(8,128)(2,1)}, u32[]{:S(2)}) copy-start(bf16[48,1536]{1,0:T(8,128)(2,1)} %copy-done.6) | copy-start | bytes 442372
  398.2 13.3 %copy-start.5 = (bf16[48,1536]{1,0:T(8,128)(2,1)S(1)}, bf16[48,1536]{1,0:T(8,128)(2,1)}, u32[]{:S(2)}) copy-start(bf16[48,1536]{1,0:T(8,128)(2,1)} %copy-done.4) | copy-start | bytes 442372
  411.6 1.4 copy-start.3
  413.0 2.6 copy-start.16
  413.0 3.1 copy-start.12
  413.0 3.1 copy-start.15
  415.6 138.6 %reduce-scatter.2.cloned.1.call-start = ((), (), s32[]{:S(2)}) async-start(), calls=%async_computation.6 | async-start | bytes 2654208 | tf_op jit(solution)/shard_map/reduce_scatter | solution.py:165
  498.7 10.5 %copy-start.1 = (f32[384]{0:T(512)}, f32[384]{0:T(512)S(1)}, u32[]{:S(2)}) copy-start(f32[384]{0:T(512)S(1)} %fusion.39) | copy-start | bytes 4612
  509.2 0.9 copy-start.2
Sparse Core Ops, SparseCore 0:
  415.7 68.4 all-reduce.2
  513.1 40.9 reduce-scatter.1
